TPU v7x, 256 devices: a whole 4x4x8 slice. The times are simulated.
256 devices in a mesh: gx: 16 (over y, z_lo), gy: 8 (over x, core), ga: 2 (over z_hi).
Axes of the slice: x: 4, y: 4, z: 8 (z_hi: 2, z_lo: 4; z = z_hi * 4 + z_lo), core: 2. Of those that a mesh axis runs over, the one named last changes fastest.
Arguments:
- thermal_anomaly: float32 [20, 1024, 4096], P(None, 'gy', ('gx', 'ga')), may hold values from -6 to 6
- sheared_current: float32 [2, 20, 1024, 4096], P(None, None, 'gy', ('gx', 'ga')), may hold values from -3 to 3
- mixing_coefficient: float32 [20, 1024, 4096], P(None, 'gy', ('gx', 'ga')), may hold values from 0.05 to 2
- surface_elevation: float32 [1024, 4096], P('gy', ('gx', 'ga')), may hold values from -2 to 2
- depth_integrated_current: float32 [2, 1024, 4096], P(None, 'gy', ('gx', 'ga')), may hold values from -3 to 3
- water_column_flag: int32 [1024, 4096], P('gy', ('gx', 'ga')), may hold values from 0 to 1
- wet_layer_counts: int32 [1024, 4096], P('gy', ('gx', 'ga')), may hold values from 1 to 20
Outputs:
- mixed: float32 [20, 1024, 4096], P(None, 'gy', ('gx', 'ga'))
- velocity_out: float32 [2, 20, 1024, 4096], P(None, None, 'gy', ('gx', 'ga'))
- height_out: float32 [1024, 4096], P('gy', ('gx', 'ga'))
- transport_out: float32 [2, 1024, 4096], P(None, 'gy', ('gx', 'ga'))
All inputs are finite; a program needn't handle non-finite values.
Results may differ from a plain program's by a relative error of at most 0.00002.
Values sent between devices are 32-bit elements; how exact they have to be, the bound alone decides.
No kernel may reach another device: no remote copies, remote signals or barrier semaphores. Data moves between devices by JAX's collectives and lax.ppermute only.
A program may use at most 64 MiB of HBM per device.

v0:
```python
import jax
import jax.numpy as jnp
from jax import lax
from jax.sharding import PartitionSpec as P

NSUB = 4


TRANSPORT_SPEED = 0.2
MIXING = 1.0
THERMAL_EXPANSION = 0.05
TIMESTEP = 0.2
SUBSTEP = 0.3
GRAVITY = 1.0


def extended(block, sides, width, periodic):
    for axis, dim in sides:
        count = lax.axis_size(axis)
        forward = [(i, i + 1) for i in range(count - 1)]
        if periodic:
            forward.append((count - 1, 0))
        backward = [(target, source) for source, target in forward]
        low = lax.ppermute(
            lax.slice_in_dim(block, block.shape[dim] - width, None, axis=dim), axis, forward
        )
        high = lax.ppermute(lax.slice_in_dim(block, 0, width, axis=dim), axis, backward)
        block = jnp.concatenate([low, block, high], axis=dim)
    return block


def mix_column(source, mixing_coefficient, water_indicator):
    depth = source.shape[0]
    coupling = [
        MIXING
        * 0.5
        * (mixing_coefficient[level] + mixing_coefficient[level + 1])
        * water_indicator[level]
        * water_indicator[level + 1]
        for level in range(depth - 1)
    ]
    ratios = []
    values = []
    for level in range(depth):
        lower = coupling[level - 1] if level > 0 else 0.0
        upper = coupling[level] if level < depth - 1 else 0.0
        diagonal = 1.0 + lower + upper
        if level == 0:
            divisor = diagonal
            carried = source[0]
        else:
            divisor = diagonal + lower * ratios[-1]
            carried = source[level] + lower * values[-1]
        ratios.append(-upper / divisor)
        values.append(carried / divisor)
    result = [values[-1]]
    for level in range(depth - 2, -1, -1):
        result.append(values[level] - ratios[level] * result[-1])
    return jnp.stack(result[::-1])


def extend(fields, width):
    fields = extended(fields, ((("gx", "ga"), 2),), width, True)
    fields = extended(fields, (("gy", 1),), width, False)
    return fields


def inner_cols(field):
    return field[:, 1:-1]


def cols_diff(field):
    return (field[:, 2:] - field[:, :-2]) * 0.5


def rows_diff(field):
    padded = jnp.pad(field, ((1, 1), (0, 0)))
    return (padded[2:, :] - padded[:-2, :]) * 0.5


def sub_step(state, consts):
    surface, east_bar, north_bar = (state[0], state[1], state[2])
    forcing_east, forcing_north, depth, wetness = (consts[0], consts[1], consts[2], consts[3])
    east_next = inner_cols(wetness) * (
        inner_cols(east_bar)
        + SUBSTEP * (-GRAVITY * inner_cols(depth) * cols_diff(surface) + inner_cols(forcing_east))
    )
    north_next = inner_cols(wetness) * (
        inner_cols(north_bar)
        + SUBSTEP
        * (
            -GRAVITY * inner_cols(depth) * inner_cols(rows_diff(surface))
            + inner_cols(forcing_north)
        )
    )
    surface_next = surface[:, 2:-2] - SUBSTEP * wetness[:, 2:-2] * (
        cols_diff(east_next) + inner_cols(rows_diff(north_next))
    )
    result = jnp.stack([surface_next, inner_cols(east_next), inner_cols(north_next)])
    return result[:, 2:-2, :]


def per_device(
    thermal_anomaly,
    sheared_current,
    mixing_coefficient,
    surface_elevation,
    depth_integrated_current,
    water_column_flag,
    wet_layer_counts,
):
    layer_thicknesses = thermal_anomaly.shape[0]
    latitudes_in_block = thermal_anomaly.shape[1]
    wetness = water_column_flag.astype(jnp.float32)
    level_ids = jnp.arange(layer_thicknesses, dtype=jnp.int32)[:, None, None]
    water_indicator = wetness[None] * (level_ids < wet_layer_counts[None]).astype(jnp.float32)
    east_current_speed = sheared_current[0]
    north_current_speed = sheared_current[1]
    east_face_transfer = east_current_speed * thermal_anomaly * water_indicator
    north_face_transfer = north_current_speed * thermal_anomaly * water_indicator
    hydrostatic_load = THERMAL_EXPANSION * jnp.cumsum(thermal_anomaly * water_indicator, axis=0)
    zonal = extended(
        jnp.stack([east_face_transfer, hydrostatic_load]), ((("gx", "ga"), 3),), 1, True
    )
    merid = extended(jnp.stack([north_face_transfer, hydrostatic_load]), (("gy", 2),), 1, False)
    longitude_slope = (zonal[..., 2:] - zonal[..., :-2]) * 0.5
    latitude_slope = (merid[..., 2:, :] - merid[..., :-2, :]) * 0.5
    carried_scalar = water_indicator * (
        thermal_anomaly - TRANSPORT_SPEED * (longitude_slope[0] + latitude_slope[0])
    )
    mixed = mix_column(carried_scalar, mixing_coefficient, water_indicator)
    row_start = lax.axis_index("gy") * latitudes_in_block
    row_index = row_start + jnp.arange(latitudes_in_block, dtype=jnp.int32)
    total_rows = latitudes_in_block * lax.axis_size("gy")
    coriolis = (0.3 + 0.4 * row_index.astype(jnp.float32) / total_rows)[:, None]
    east_new = water_indicator * (
        east_current_speed + TIMESTEP * (coriolis * north_current_speed - longitude_slope[1])
    )
    north_new = water_indicator * (
        north_current_speed + TIMESTEP * (-coriolis * east_current_speed - latitude_slope[1])
    )
    forcing_east = (
        jnp.sum(water_indicator * (east_new - east_current_speed), axis=0) / layer_thicknesses
    )
    forcing_north = (
        jnp.sum(water_indicator * (north_new - north_current_speed), axis=0) / layer_thicknesses
    )
    depth = wetness * wet_layer_counts.astype(jnp.float32) / layer_thicknesses
    band = jnp.stack(
        [
            surface_elevation,
            depth_integrated_current[0],
            depth_integrated_current[1],
            forcing_east,
            forcing_north,
            depth,
            wetness,
        ]
    )
    consts = extend(band[3:], 2)
    state = band[:3]
    for step in range(NSUB):
        state = sub_step(extend(state, 2), consts)
    surface = state[0]
    east_bar = state[1]
    north_bar = state[2]
    count = jnp.maximum(jnp.sum(water_indicator, axis=0), 1.0)
    east_out = water_indicator * (
        east_new - jnp.sum(water_indicator * east_new, axis=0) / count + east_bar
    )
    north_out = water_indicator * (
        north_new - jnp.sum(water_indicator * north_new, axis=0) / count + north_bar
    )
    return (mixed, jnp.stack([east_out, north_out]), surface, jnp.stack([east_bar, north_bar]))


def solution(mesh):
    placed = (
        P(None, "gy", ("gx", "ga")),
        P(None, None, "gy", ("gx", "ga")),
        P(None, "gy", ("gx", "ga")),
        P("gy", ("gx", "ga")),
        P(None, "gy", ("gx", "ga")),
        P("gy", ("gx", "ga")),
        P("gy", ("gx", "ga")),
    )
    return jax.shard_map(
        per_device,
        mesh=mesh,
        in_specs=placed,
        out_specs=(
            P(None, "gy", ("gx", "ga")),
            P(None, None, "gy", ("gx", "ga")),
            P("gy", ("gx", "ga")),
            P(None, "gy", ("gx", "ga")),
        ),
        check_vma=False,
    )
```

profile of v0, /device:TPU:33, one launch (start us, length us, event | category | flops | bytes accessed | tf_op | source)
XLA Modules:
  0.0 218.6 jit_solution(4494156320935481956)
XLA Ops:
  0.6 0.9 convert_bitcast_fusion
  1.5 1.7 broadcast_multiply_fusion
  3.6 3.3 %fusion.9 = (f32[1,20,128,128]{3,2,1,0:T(8,128)S(1)}, f32[1,20,128,128]{3,2,1,0:T(8,128)}) fusion(f32[20,128,128]{2,1,0:T(8,128)} %param.7, f32[2,20,128,128]{3,2,1,0:T(8,128)S(1)} %copy-done, f32[128,128]{1,0:T(8,128)S(1)} %get-tuple-element.153, s32[128,128]{1,0:T(8,128)S(1)} %copy-done.4), kind=kLoop, calls=%fused_computation.37 | loop fusion | flops 1966080 | bytes 6684672 | tf_op jit(solution)/shard_map/stack | solution.py:123
  6.9 3.4 %fusion = (f32[2,20,128,1]{3,2,1,0:T(8,128)}, f32[2,20,128,1]{3,2,1,0:T(8,128)}) fusion(f32[1,20,128,128]{3,2,1,0:T(8,128)S(1)} %broadcast_multiply_fusion, f32[1,20,128,128]{3,2,1,0:T(8,128)S(1)} %get-tuple-element.64), kind=kLoop, calls=%fused_computation.13 | loop fusion | flops 10240 | bytes 2662400 | tf_op jit(solution)/shard_map/stack | solution.py:123
  10.3 2.5 %copy.11 = f32[2,20,128,1]{2,0,3,1:T(2,128)S(1)} copy(f32[2,20,128,1]{3,2,1,0:T(8,128)} %get-tuple-element.71) | data formatting | bytes 40960 | tf_op jit(solution)/shard_map/slice | solution.py:27
  12.8 5.6 %collective-permute-start = (f32[2,20,128,1]{2,0,3,1:T(2,128)S(1)}, f32[2,20,128,1]{2,0,3,1:T(2,128)S(1)}, u32[]{:S(2)}, u32[]{:S(2)}) collective-permute-start(f32[2,20,128,1]{2,0,3,1:T(2,128)S(1)} %copy.11), channel_id=1, source_target_pairs={{1,0},{16,1},{17,16},{32,17},{33,32},{48,33},{49,48},{64,49},{65,6... | collective-permute-start | bytes 61448 | tf_op jit(solution)/shard_map/ppermute | solution.py:27
  18.4 3.1 %copy.13 = f32[2,20,128,1]{2,0,3,1:T(2,128)} copy(f32[2,20,128,1]{3,2,1,0:T(8,128)} %get-tuple-element.72) | data formatting | bytes 40960 | tf_op jit(solution)/shard_map/slice | solution.py:25
  22.0 1.7 fusion.123
  23.7 2.9 %collective-permute-start.2 = (f32[2,20,1,128]{3,2,1,0:T(1,128)}, f32[2,20,1,128]{3,2,1,0:T(1,128)S(1)}, u32[]{:S(2)}, u32[]{:S(2)}) collective-permute-start(f32[2,20,1,128]{3,2,1,0:T(1,128)} %get-tuple-element.73), channel_id=1, source_target_pairs={{2,0},{4,2},{6,4},{8,6},{10,8},{12,10},{14,12},{3,1},{5,3},{7,5},{... | collective-permute-start | bytes 61448 | tf_op jit(solution)/shard_map/ppermute | solution.py:27
  26.6 0.8 slice_maximum_fusion
  27.4 4.7 %collective-permute-start.8 = (f32[3,128,2]{2,1,0:T(8,128)}, f32[3,128,2]{2,1,0:T(8,128)S(1)}, u32[]{:S(2)}, u32[]{:S(2)}) collective-permute-start(f32[3,128,2]{2,1,0:T(8,128)} %get-tuple-element.119), channel_id=1, source_target_pairs={{0,1},{1,16},{16,17},{17,32},{32,33},{33,48},{48,49},{49,64},{64,6... | collective-permute-start | bytes 9224 | tf_op jit(solution)/shard_map/ppermute | solution.py:24
  32.1 21.9 %collective-permute-done.8 = f32[3,128,2]{2,1,0:T(8,128)S(1)} collective-permute-done((f32[3,128,2]{2,1,0:T(8,128)}, f32[3,128,2]{2,1,0:T(8,128)S(1)}, u32[]{:S(2)}, u32[]{:S(2)}) %collective-permute-start.8) | collective-permute-done | bytes 3104 | tf_op jit(solution)/shard_map/ppermute | solution.py:24
  54.1 3.7 %collective-permute-start.10 = (f32[3,2,132]{2,1,0:T(2,128)S(1)}, f32[3,2,132]{2,1,0:T(2,128)S(1)}, u32[]{:S(2)}, u32[]{:S(2)}) collective-permute-start(f32[3,2,132]{2,1,0:T(2,128)S(1)} %get-tuple-element.85), channel_id=1, source_target_pairs={{0,2},{2,4},{4,6},{6,8},{8,10},{10,12},{12,14},{1,3},{3,5},{5,7},{... | collective-permute-start | bytes 9512 | tf_op jit(solution)/shard_map/ppermute | solution.py:24
  57.9 1.9 collective-permute-start.11
  59.8 3.6 %collective-permute-start.3 = (f32[2,20,1,128]{3,2,1,0:T(1,128)}, f32[2,20,1,128]{3,2,1,0:T(1,128)}, u32[]{:S(2)}, u32[]{:S(2)}) collective-permute-start(f32[2,20,1,128]{3,2,1,0:T(1,128)} %get-tuple-element.74), channel_id=1, source_target_pairs={{0,2},{2,4},{4,6},{6,8},{8,10},{10,12},{12,14},{1,3},{3,5},{5,7},{... | collective-permute-start | bytes 61448 | tf_op jit(solution)/shard_map/ppermute | solution.py:24
  63.8 0.7 pad_slice_fusion.18
  64.4 2.3 %copy.12 = f32[2,20,128,1]{3,2,1,0:T(8,128)} copy(f32[2,20,128,1]{2,0,3,1:T(2,128)S(1)} %collective-permute-done) | data formatting | bytes 40960 | tf_op jit(solution)/shard_map/ppermute | solution.py:27
  66.7 3.0 %copy.14 = f32[2,20,128,1]{3,2,1,0:T(8,128)} copy(f32[2,20,128,1]{2,0,3,1:T(2,128)} %collective-permute-done.1) | data formatting | bytes 40960 | tf_op jit(solution)/shard_map/ppermute | solution.py:24
  69.7 8.9 %fusion.4 = (f32[2,20,128,128]{3,2,1,0:T(8,128)S(1)}, f32[2,20,128,128]{3,2,1,0:T(8,128)S(1)}) fusion(f32[2,20,128,1]{3,2,1,0:T(8,128)} %copy.14, f32[1,20,128,128]{3,2,1,0:T(8,128)} %copy-done.1, f32[1,20,128,128]{3,2,1,0:T(8,128)} %copy-done.2, f32[2,20,128,1]{3,2,1,0:T(8,128)} %copy.12, f32[1,20,128,128]{3,2,1,0:T(8,128)} %get-tuple-element.65, ...), kind=kLoop, calls=%fused_computation.22 | loop fusion | flops 7864320 | bytes 9256960 | tf_op jit(solution)/shard_map/mul | solution.py:126
  78.6 1.2 select_multiply_fusion.2
  79.9 0.7 fusion.15
  80.7 1.2 collective-permute-start.4
  81.9 3.4 %collective-permute-start.5 = (f32[4,128,2]{2,1,0:T(8,128)S(1)}, f32[4,128,2]{2,1,0:T(8,128)S(1)}, u32[]{:S(2)}, u32[]{:S(2)}) collective-permute-start(f32[4,128,2]{2,1,0:T(8,128)S(1)} %get-tuple-element.112), channel_id=1, source_target_pairs={{1,0},{16,1},{17,16},{32,17},{33,32},{48,33},{49,48},{64,49},{65,6... | collective-permute-start | bytes 12296 | tf_op jit(solution)/shard_map/ppermute | solution.py:27
  85.3 0.6 fusion.105
  86.5 24.3 %collective-permute-done.4 = f32[4,128,2]{2,1,0:T(8,128)S(1)} collective-permute-done((f32[4,128,2]{2,1,0:T(8,128)S(1)}, f32[4,128,2]{2,1,0:T(8,128)S(1)}, u32[]{:S(2)}, u32[]{:S(2)}) %collective-permute-start.4) | collective-permute-done | bytes 4128 | tf_op jit(solution)/shard_map/ppermute | solution.py:24
  110.9 2.9 %collective-permute-start.6 = (f32[4,2,132]{2,1,0:T(2,128)S(1)}, f32[4,2,132]{2,1,0:T(2,128)S(1)}, u32[]{:S(2)}, u32[]{:S(2)}) collective-permute-start(f32[4,2,132]{2,1,0:T(2,128)S(1)} %get-tuple-element.77), channel_id=1, source_target_pairs={{0,2},{2,4},{4,6},{6,8},{8,10},{10,12},{12,14},{1,3},{3,5},{5,7},{... | collective-permute-start | bytes 12680 | tf_op jit(solution)/shard_map/ppermute | solution.py:24
  113.8 1.9 collective-permute-start.7
  115.8 3.0 %collective-permute-done.7 = f32[4,2,132]{2,1,0:T(2,128)S(1)} collective-permute-done((f32[4,2,132]{2,1,0:T(2,128)S(1)}, f32[4,2,132]{2,1,0:T(2,128)S(1)}, u32[]{:S(2)}, u32[]{:S(2)}) %collective-permute-start.7) | collective-permute-done | bytes 4256 | tf_op jit(solution)/shard_map/ppermute | solution.py:27
  120.1 4.5 %collective-permute-start.13 = (f32[3,128,2]{2,1,0:T(8,128)S(1)}, f32[3,128,2]{2,1,0:T(8,128)S(1)}, u32[]{:S(2)}, u32[]{:S(2)}) collective-permute-start(f32[3,128,2]{2,1,0:T(8,128)S(1)} %get-tuple-element.118), channel_id=1, source_target_pairs={{1,0},{16,1},{17,16},{32,17},{33,32},{48,33},{49,48},{64,49},{65,6... | collective-permute-start | bytes 9224 | tf_op jit(solution)/shard_map/ppermute | solution.py:27
  124.6 16.3 %collective-permute-done.12 = f32[3,128,2]{2,1,0:T(8,128)S(1)} collective-permute-done((f32[3,128,2]{2,1,0:T(8,128)S(1)}, f32[3,128,2]{2,1,0:T(8,128)S(1)}, u32[]{:S(2)}, u32[]{:S(2)}) %collective-permute-start.12) | collective-permute-done | bytes 3104 | tf_op jit(solution)/shard_map/ppermute | solution.py:24
  141.0 3.9 %collective-permute-start.14 = (f32[3,2,132]{2,1,0:T(2,128)S(1)}, f32[3,2,132]{2,1,0:T(2,128)S(1)}, u32[]{:S(2)}, u32[]{:S(2)}) collective-permute-start(f32[3,2,132]{2,1,0:T(2,128)S(1)} %get-tuple-element.83), channel_id=1, source_target_pairs={{0,2},{2,4},{4,6},{6,8},{8,10},{10,12},{12,14},{1,3},{3,5},{5,7},{... | collective-permute-start | bytes 9512 | tf_op jit(solution)/shard_map/ppermute | solution.py:24
  145.0 1.9 collective-permute-start.15
  146.9 3.0 %collective-permute-done.15 = f32[3,2,132]{2,1,0:T(2,128)S(1)} collective-permute-done((f32[3,2,132]{2,1,0:T(2,128)S(1)}, f32[3,2,132]{2,1,0:T(2,128)S(1)}, u32[]{:S(2)}, u32[]{:S(2)}) %collective-permute-start.15) | collective-permute-done | bytes 3200 | tf_op jit(solution)/shard_map/ppermute | solution.py:27
  151.1 2.0 collective-permute-start.16
  153.1 2.5 %collective-permute-start.17 = (f32[3,128,2]{2,1,0:T(8,128)S(1)}, f32[3,128,2]{2,1,0:T(8,128)S(1)}, u32[]{:S(2)}, u32[]{:S(2)}) collective-permute-start(f32[3,128,2]{2,1,0:T(8,128)S(1)} %get-tuple-element.116), channel_id=1, source_target_pairs={{1,0},{16,1},{17,16},{32,17},{33,32},{48,33},{49,48},{64,49},{65,6... | collective-permute-start | bytes 9224 | tf_op jit(solution)/shard_map/ppermute | solution.py:27
  155.7 18.0 %collective-permute-done.16 = f32[3,128,2]{2,1,0:T(8,128)S(1)} collective-permute-done((f32[3,128,2]{2,1,0:T(8,128)S(1)}, f32[3,128,2]{2,1,0:T(8,128)S(1)}, u32[]{:S(2)}, u32[]{:S(2)}) %collective-permute-start.16) | collective-permute-done | bytes 3104 | tf_op jit(solution)/shard_map/ppermute | solution.py:24
  173.8 4.1 %collective-permute-start.18 = (f32[3,2,132]{2,1,0:T(2,128)S(1)}, f32[3,2,132]{2,1,0:T(2,128)S(1)}, u32[]{:S(2)}, u32[]{:S(2)}) collective-permute-start(f32[3,2,132]{2,1,0:T(2,128)S(1)} %get-tuple-element.81), channel_id=1, source_target_pairs={{0,2},{2,4},{4,6},{6,8},{8,10},{10,12},{12,14},{1,3},{3,5},{5,7},{... | collective-permute-start | bytes 9512 | tf_op jit(solution)/shard_map/ppermute | solution.py:24
  177.9 1.9 collective-permute-start.19
  180.0 2.9 %collective-permute-done.19 = f32[3,2,132]{2,1,0:T(2,128)S(1)} collective-permute-done((f32[3,2,132]{2,1,0:T(2,128)S(1)}, f32[3,2,132]{2,1,0:T(2,128)S(1)}, u32[]{:S(2)}, u32[]{:S(2)}) %collective-permute-start.19) | collective-permute-done | bytes 3200 | tf_op jit(solution)/shard_map/ppermute | solution.py:27
  184.4 4.2 %collective-permute-start.21 = (f32[3,128,2]{2,1,0:T(8,128)S(1)}, f32[3,128,2]{2,1,0:T(8,128)S(1)}, u32[]{:S(2)}, u32[]{:S(2)}) collective-permute-start(f32[3,128,2]{2,1,0:T(8,128)S(1)} %get-tuple-element.114), channel_id=1, source_target_pairs={{1,0},{16,1},{17,16},{32,17},{33,32},{48,33},{49,48},{64,49},{65,6... | collective-permute-start | bytes 9224 | tf_op jit(solution)/shard_map/ppermute | solution.py:27
  188.7 16.3 %collective-permute-done.20 = f32[3,128,2]{2,1,0:T(8,128)S(1)} collective-permute-done((f32[3,128,2]{2,1,0:T(8,128)S(1)}, f32[3,128,2]{2,1,0:T(8,128)S(1)}, u32[]{:S(2)}, u32[]{:S(2)}) %collective-permute-start.20) | collective-permute-done | bytes 3104 | tf_op jit(solution)/shard_map/ppermute | solution.py:24
  205.1 3.6 %collective-permute-start.22 = (f32[3,2,132]{2,1,0:T(2,128)S(1)}, f32[3,2,132]{2,1,0:T(2,128)S(1)}, u32[]{:S(2)}, u32[]{:S(2)}) collective-permute-start(f32[3,2,132]{2,1,0:T(2,128)S(1)} %get-tuple-element.79), channel_id=1, source_target_pairs={{0,2},{2,4},{4,6},{6,8},{8,10},{10,12},{12,14},{1,3},{3,5},{5,7},{... | collective-permute-start | bytes 9512 | tf_op jit(solution)/shard_map/ppermute | solution.py:24
  208.7 1.9 collective-permute-start.23
  210.7 3.0 %collective-permute-done.23 = f32[3,2,132]{2,1,0:T(2,128)S(1)} collective-permute-done((f32[3,2,132]{2,1,0:T(2,128)S(1)}, f32[3,2,132]{2,1,0:T(2,128)S(1)}, u32[]{:S(2)}, u32[]{:S(2)}) %collective-permute-start.23) | collective-permute-done | bytes 3200 | tf_op jit(solution)/shard_map/ppermute | solution.py:27
  214.8 0.6 slice_bitcast_fusion.24
  215.4 0.7 pad_maximum_fusion.20
  216.1 0.8 select_multiply_fusion.12
  216.9 1.7 pad_maximum_fusion.9
  (113 shorter events, 7.5 us)
Async XLA Ops:
  1.5 2.2 copy-start
  1.5 2.1 copy-start.4
  3.6 3.3 %copy-start.1 = (f32[1,20,128,128]{3,2,1,0:T(8,128)}, f32[1,20,128,128]{3,2,1,0:T(8,128)S(1)}, u32[]{:S(2)}) copy-start(f32[1,20,128,128]{3,2,1,0:T(8,128)S(1)} %broadcast_multiply_fusion) | copy-start | bytes 3932164
  6.9 3.4 %copy-start.2 = (f32[1,20,128,128]{3,2,1,0:T(8,128)}, f32[1,20,128,128]{3,2,1,0:T(8,128)S(1)}, u32[]{:S(2)}) copy-start(f32[1,20,128,128]{3,2,1,0:T(8,128)S(1)} %get-tuple-element.64) | copy-start | bytes 3932164
  12.8 51.6 %collective-permute-start = (f32[2,20,128,1]{2,0,3,1:T(2,128)S(1)}, f32[2,20,128,1]{2,0,3,1:T(2,128)S(1)}, u32[]{:S(2)}, u32[]{:S(2)}) collective-permute-start(f32[2,20,128,1]{2,0,3,1:T(2,128)S(1)} %copy.11), channel_id=1, source_target_pairs={{1,0},{16,1},{17,16},{32,17},{33,32},{48,33},{49,48},{64,49},{65,6... | collective-permute-start | bytes 61448 | tf_op jit(solution)/shard_map/ppermute | solution.py:27
  21.5 45.2 %collective-permute-start.1 = (f32[2,20,128,1]{2,0,3,1:T(2,128)}, f32[2,20,128,1]{2,0,3,1:T(2,128)}, u32[]{:S(2)}, u32[]{:S(2)}) collective-permute-start(f32[2,20,128,1]{2,0,3,1:T(2,128)} %copy.13), channel_id=1, source_target_pairs={{0,1},{1,16},{16,17},{17,32},{32,33},{33,48},{48,49},{49,64},{64,6... | collective-permute-start | bytes 61448 | tf_op jit(solution)/shard_map/ppermute | solution.py:24
  22.0 4.6 %copy-start.6 = (f32[2,128,128]{2,1,0:T(8,128)S(1)}, f32[2,128,128]{2,1,0:T(8,128)}, u32[]{:S(2)}) copy-start(f32[2,128,128]{2,1,0:T(8,128)} %param.11) | copy-start | bytes 393220
  22.0 4.6 %copy-start.7 = (f32[128,128]{1,0:T(8,128)S(1)}, f32[128,128]{1,0:T(8,128)}, u32[]{:S(2)}) copy-start(f32[128,128]{1,0:T(8,128)} %param.10) | copy-start | bytes 196612
  22.0 10.1 %copy-start.9 = (s32[128,128]{1,0:T(8,128)S(1)}, s32[128,128]{1,0:T(8,128)}, u32[]{:S(2)}) copy-start(s32[128,128]{1,0:T(8,128)} %param.12) | copy-start | bytes 196612
  23.7 46.0 %collective-permute-start.2 = (f32[2,20,1,128]{3,2,1,0:T(1,128)}, f32[2,20,1,128]{3,2,1,0:T(1,128)S(1)}, u32[]{:S(2)}, u32[]{:S(2)}) collective-permute-start(f32[2,20,1,128]{3,2,1,0:T(1,128)} %get-tuple-element.73), channel_id=1, source_target_pairs={{2,0},{4,2},{6,4},{8,6},{10,8},{12,10},{14,12},{3,1},{5,3},{7,5},{... | collective-permute-start | bytes 61448 | tf_op jit(solution)/shard_map/ppermute | solution.py:27
  27.4 26.7 %collective-permute-start.8 = (f32[3,128,2]{2,1,0:T(8,128)}, f32[3,128,2]{2,1,0:T(8,128)S(1)}, u32[]{:S(2)}, u32[]{:S(2)}) collective-permute-start(f32[3,128,2]{2,1,0:T(8,128)} %get-tuple-element.119), channel_id=1, source_target_pairs={{0,1},{1,16},{16,17},{17,32},{32,33},{33,48},{48,49},{49,64},{64,6... | collective-permute-start | bytes 9224 | tf_op jit(solution)/shard_map/ppermute | solution.py:24
  32.1 21.9 %collective-permute-start.9 = (f32[3,128,2]{2,1,0:T(8,128)}, f32[3,128,2]{2,1,0:T(8,128)S(1)}, u32[]{:S(2)}, u32[]{:S(2)}) collective-permute-start(f32[3,128,2]{2,1,0:T(8,128)} %get-tuple-element.120), channel_id=1, source_target_pairs={{1,0},{16,1},{17,16},{32,17},{33,32},{48,33},{49,48},{64,49},{65,6... | collective-permute-start | bytes 9224 | tf_op jit(solution)/shard_map/ppermute | solution.py:27
  54.1 5.7 %collective-permute-start.10 = (f32[3,2,132]{2,1,0:T(2,128)S(1)}, f32[3,2,132]{2,1,0:T(2,128)S(1)}, u32[]{:S(2)}, u32[]{:S(2)}) collective-permute-start(f32[3,2,132]{2,1,0:T(2,128)S(1)} %get-tuple-element.85), channel_id=1, source_target_pairs={{0,2},{2,4},{4,6},{6,8},{8,10},{10,12},{12,14},{1,3},{3,5},{5,7},{... | collective-permute-start | bytes 9512 | tf_op jit(solution)/shard_map/ppermute | solution.py:24
  57.9 5.6 %collective-permute-start.11 = (f32[3,2,132]{2,1,0:T(2,128)S(1)}, f32[3,2,132]{2,1,0:T(2,128)S(1)}, u32[]{:S(2)}, u32[]{:S(2)}) collective-permute-start(f32[3,2,132]{2,1,0:T(2,128)S(1)} %get-tuple-element.86), channel_id=1, source_target_pairs={{2,0},{4,2},{6,4},{8,6},{10,8},{12,10},{14,12},{3,1},{5,3},{7,5},{... | collective-permute-start | bytes 9512 | tf_op jit(solution)/shard_map/ppermute | solution.py:27
  59.8 9.9 %collective-permute-start.3 = (f32[2,20,1,128]{3,2,1,0:T(1,128)}, f32[2,20,1,128]{3,2,1,0:T(1,128)}, u32[]{:S(2)}, u32[]{:S(2)}) collective-permute-start(f32[2,20,1,128]{3,2,1,0:T(1,128)} %get-tuple-element.74), channel_id=1, source_target_pairs={{0,2},{2,4},{4,6},{6,8},{8,10},{10,12},{12,14},{1,3},{3,5},{5,7},{... | collective-permute-start | bytes 61448 | tf_op jit(solution)/shard_map/ppermute | solution.py:24
  69.7 8.9 %copy-start.3 = (f32[20,128,128]{2,1,0:T(8,128)S(1)}, f32[20,128,128]{2,1,0:T(8,128)}, u32[]{:S(2)}) copy-start(f32[20,128,128]{2,1,0:T(8,128)} %param.7) | copy-start | bytes 3932164
  80.5 4.8 %copy-start.5 = (f32[20,128,128]{2,1,0:T(8,128)S(1)}, f32[20,128,128]{2,1,0:T(8,128)}, u32[]{:S(2)}) copy-start(f32[20,128,128]{2,1,0:T(8,128)} %param.9) | copy-start | bytes 3932164
  80.7 30.0 %collective-permute-start.4 = (f32[4,128,2]{2,1,0:T(8,128)S(1)}, f32[4,128,2]{2,1,0:T(8,128)S(1)}, u32[]{:S(2)}, u32[]{:S(2)}) collective-permute-start(f32[4,128,2]{2,1,0:T(8,128)S(1)} %get-tuple-element.111), channel_id=1, source_target_pairs={{0,1},{1,16},{16,17},{17,32},{32,33},{33,48},{48,49},{49,64},{64,6... | collective-permute-start | bytes 12296 | tf_op jit(solution)/shard_map/ppermute | solution.py:24
  81.9 28.9 %collective-permute-start.5 = (f32[4,128,2]{2,1,0:T(8,128)S(1)}, f32[4,128,2]{2,1,0:T(8,128)S(1)}, u32[]{:S(2)}, u32[]{:S(2)}) collective-permute-start(f32[4,128,2]{2,1,0:T(8,128)S(1)} %get-tuple-element.112), channel_id=1, source_target_pairs={{1,0},{16,1},{17,16},{32,17},{33,32},{48,33},{49,48},{64,49},{65,6... | collective-permute-start | bytes 12296 | tf_op jit(solution)/shard_map/ppermute | solution.py:27
  110.9 4.9 %collective-permute-start.6 = (f32[4,2,132]{2,1,0:T(2,128)S(1)}, f32[4,2,132]{2,1,0:T(2,128)S(1)}, u32[]{:S(2)}, u32[]{:S(2)}) collective-permute-start(f32[4,2,132]{2,1,0:T(2,128)S(1)} %get-tuple-element.77), channel_id=1, source_target_pairs={{0,2},{2,4},{4,6},{6,8},{8,10},{10,12},{12,14},{1,3},{3,5},{5,7},{... | collective-permute-start | bytes 12680 | tf_op jit(solution)/shard_map/ppermute | solution.py:24
  113.8 5.0 %collective-permute-start.7 = (f32[4,2,132]{2,1,0:T(2,128)S(1)}, f32[4,2,132]{2,1,0:T(2,128)S(1)}, u32[]{:S(2)}, u32[]{:S(2)}) collective-permute-start(f32[4,2,132]{2,1,0:T(2,128)S(1)} %get-tuple-element.78), channel_id=1, source_target_pairs={{2,0},{4,2},{6,4},{8,6},{10,8},{12,10},{14,12},{3,1},{5,3},{7,5},{... | collective-permute-start | bytes 12680 | tf_op jit(solution)/shard_map/ppermute | solution.py:27
  115.7 3.4 %copy-start.8 = (f32[132,132]{1,0:T(8,128)S(1)}, f32[132,132]{1,0:T(8,128)}, u32[]{:S(2)}) copy-start(f32[132,132]{1,0:T(8,128)} %get-tuple-element.144) | copy-start | bytes 209092
  120.0 20.9 %collective-permute-start.12 = (f32[3,128,2]{2,1,0:T(8,128)S(1)}, f32[3,128,2]{2,1,0:T(8,128)S(1)}, u32[]{:S(2)}, u32[]{:S(2)}) collective-permute-start(f32[3,128,2]{2,1,0:T(8,128)S(1)} %get-tuple-element.117), channel_id=1, source_target_pairs={{0,1},{1,16},{16,17},{17,32},{32,33},{33,48},{48,49},{49,64},{64,6... | collective-permute-start | bytes 9224 | tf_op jit(solution)/shard_map/ppermute | solution.py:24
  120.1 20.8 %collective-permute-start.13 = (f32[3,128,2]{2,1,0:T(8,128)S(1)}, f32[3,128,2]{2,1,0:T(8,128)S(1)}, u32[]{:S(2)}, u32[]{:S(2)}) collective-permute-start(f32[3,128,2]{2,1,0:T(8,128)S(1)} %get-tuple-element.118), channel_id=1, source_target_pairs={{1,0},{16,1},{17,16},{32,17},{33,32},{48,33},{49,48},{64,49},{65,6... | collective-permute-start | bytes 9224 | tf_op jit(solution)/shard_map/ppermute | solution.py:27
  141.0 5.9 %collective-permute-start.14 = (f32[3,2,132]{2,1,0:T(2,128)S(1)}, f32[3,2,132]{2,1,0:T(2,128)S(1)}, u32[]{:S(2)}, u32[]{:S(2)}) collective-permute-start(f32[3,2,132]{2,1,0:T(2,128)S(1)} %get-tuple-element.83), channel_id=1, source_target_pairs={{0,2},{2,4},{4,6},{6,8},{8,10},{10,12},{12,14},{1,3},{3,5},{5,7},{... | collective-permute-start | bytes 9512 | tf_op jit(solution)/shard_map/ppermute | solution.py:24
  145.0 4.9 %collective-permute-start.15 = (f32[3,2,132]{2,1,0:T(2,128)S(1)}, f32[3,2,132]{2,1,0:T(2,128)S(1)}, u32[]{:S(2)}, u32[]{:S(2)}) collective-permute-start(f32[3,2,132]{2,1,0:T(2,128)S(1)} %get-tuple-element.84), channel_id=1, source_target_pairs={{2,0},{4,2},{6,4},{8,6},{10,8},{12,10},{14,12},{3,1},{5,3},{7,5},{... | collective-permute-start | bytes 9512 | tf_op jit(solution)/shard_map/ppermute | solution.py:27
  151.1 22.6 %collective-permute-start.16 = (f32[3,128,2]{2,1,0:T(8,128)S(1)}, f32[3,128,2]{2,1,0:T(8,128)S(1)}, u32[]{:S(2)}, u32[]{:S(2)}) collective-permute-start(f32[3,128,2]{2,1,0:T(8,128)S(1)} %get-tuple-element.115), channel_id=1, source_target_pairs={{0,1},{1,16},{16,17},{17,32},{32,33},{33,48},{48,49},{49,64},{64,6... | collective-permute-start | bytes 9224 | tf_op jit(solution)/shard_map/ppermute | solution.py:24
  153.1 20.6 %collective-permute-start.17 = (f32[3,128,2]{2,1,0:T(8,128)S(1)}, f32[3,128,2]{2,1,0:T(8,128)S(1)}, u32[]{:S(2)}, u32[]{:S(2)}) collective-permute-start(f32[3,128,2]{2,1,0:T(8,128)S(1)} %get-tuple-element.116), channel_id=1, source_target_pairs={{1,0},{16,1},{17,16},{32,17},{33,32},{48,33},{49,48},{64,49},{65,6... | collective-permute-start | bytes 9224 | tf_op jit(solution)/shard_map/ppermute | solution.py:27
  173.8 6.2 %collective-permute-start.18 = (f32[3,2,132]{2,1,0:T(2,128)S(1)}, f32[3,2,132]{2,1,0:T(2,128)S(1)}, u32[]{:S(2)}, u32[]{:S(2)}) collective-permute-start(f32[3,2,132]{2,1,0:T(2,128)S(1)} %get-tuple-element.81), channel_id=1, source_target_pairs={{0,2},{2,4},{4,6},{6,8},{8,10},{10,12},{12,14},{1,3},{3,5},{5,7},{... | collective-permute-start | bytes 9512 | tf_op jit(solution)/shard_map/ppermute | solution.py:24
  177.9 4.9 %collective-permute-start.19 = (f32[3,2,132]{2,1,0:T(2,128)S(1)}, f32[3,2,132]{2,1,0:T(2,128)S(1)}, u32[]{:S(2)}, u32[]{:S(2)}) collective-permute-start(f32[3,2,132]{2,1,0:T(2,128)S(1)} %get-tuple-element.82), channel_id=1, source_target_pairs={{2,0},{4,2},{6,4},{8,6},{10,8},{12,10},{14,12},{3,1},{5,3},{7,5},{... | collective-permute-start | bytes 9512 | tf_op jit(solution)/shard_map/ppermute | solution.py:27
  184.1 20.9 %collective-permute-start.20 = (f32[3,128,2]{2,1,0:T(8,128)S(1)}, f32[3,128,2]{2,1,0:T(8,128)S(1)}, u32[]{:S(2)}, u32[]{:S(2)}) collective-permute-start(f32[3,128,2]{2,1,0:T(8,128)S(1)} %get-tuple-element.113), channel_id=1, source_target_pairs={{0,1},{1,16},{16,17},{17,32},{32,33},{33,48},{48,49},{49,64},{64,6... | collective-permute-start | bytes 9224 | tf_op jit(solution)/shard_map/ppermute | solution.py:24
  184.4 20.6 %collective-permute-start.21 = (f32[3,128,2]{2,1,0:T(8,128)S(1)}, f32[3,128,2]{2,1,0:T(8,128)S(1)}, u32[]{:S(2)}, u32[]{:S(2)}) collective-permute-start(f32[3,128,2]{2,1,0:T(8,128)S(1)} %get-tuple-element.114), channel_id=1, source_target_pairs={{1,0},{16,1},{17,16},{32,17},{33,32},{48,33},{49,48},{64,49},{65,6... | collective-permute-start | bytes 9224 | tf_op jit(solution)/shard_map/ppermute | solution.py:27
  188.7 25.3 %copy-start.10 = (f32[20,128,128]{2,1,0:T(8,128)}, f32[20,128,128]{2,1,0:T(8,128)S(1)}, u32[]{:S(2)}) copy-start(f32[20,128,128]{2,1,0:T(8,128)S(1)} %constant_dynamic-update-slice_fusion) | copy-start | bytes 3932164
  205.1 5.6 %collective-permute-start.22 = (f32[3,2,132]{2,1,0:T(2,128)S(1)}, f32[3,2,132]{2,1,0:T(2,128)S(1)}, u32[]{:S(2)}, u32[]{:S(2)}) collective-permute-start(f32[3,2,132]{2,1,0:T(2,128)S(1)} %get-tuple-element.79), channel_id=1, source_target_pairs={{0,2},{2,4},{4,6},{6,8},{8,10},{10,12},{12,14},{1,3},{3,5},{5,7},{... | collective-permute-start | bytes 9512 | tf_op jit(solution)/shard_map/ppermute | solution.py:24
  208.7 4.9 %collective-permute-start.23 = (f32[3,2,132]{2,1,0:T(2,128)S(1)}, f32[3,2,132]{2,1,0:T(2,128)S(1)}, u32[]{:S(2)}, u32[]{:S(2)}) collective-permute-start(f32[3,2,132]{2,1,0:T(2,128)S(1)} %get-tuple-element.80), channel_id=1, source_target_pairs={{2,0},{4,2},{6,4},{8,6},{10,8},{12,10},{14,12},{3,1},{5,3},{7,5},{... | collective-permute-start | bytes 9512 | tf_op jit(solution)/shard_map/ppermute | solution.py:27
where the time goes:
time: 219 us
  waiting for transfers between devices  109 us (50%)
  starting transfers between devices  63.5 us (29%)
  other arithmetic  31.1 us (14%)
  local copies, waits for them, and re-layouts  13.9 us (6%)
    ppermute x12, waiting for transfers between devices, extended(): lax.ppermute(lax.slice_in_dim(block, block.shape[dim] - width, None, axis...  96.9 us
    ppermute x12, starting transfers between devices, extended(): lax.ppermute(lax.slice_in_dim(block, 0, width, axis=dim), axis, backward)  32.7 us
    ppermute x12, starting transfers between devices, extended(): lax.ppermute(lax.slice_in_dim(block, block.shape[dim] - width, None, axis...  30.8 us
    ppermute x12, waiting for transfers between devices, extended(): lax.ppermute(lax.slice_in_dim(block, 0, width, axis=dim), axis, backward)  11.9 us
    mul x1, other arithmetic, per_device(): longitude_slope = (zonal[..., 2:] - zonal[..., :-2]) * 0.5  8.92 us
    another operation x2, other arithmetic, per_device(): jnp.stack([east_face_transfer, hydrostatic_load])  6.65 us
  transfers between devices with their start and end apart: 24, of which 9 were waited for; matrix products, arithmetic and copies ran while one was open for 6% of the time, Pallas kernels for 0%

commit v1 on v0

v1 whole, which is shorter than its diff:
```python
import functools

import jax
import jax.numpy as jnp
from jax import lax
from jax.experimental import pallas as pl
from jax.experimental.pallas import tpu as pltpu
from jax.sharding import PartitionSpec as P

NSUB = 4
W = 8
TRANSPORT_SPEED = 0.2
MIXING = 1.0
THERMAL_EXPANSION = 0.05
TIMESTEP = 0.2
SUBSTEP = 0.3
GRAVITY = 1.0

AXES = ("gx", "gy", "ga")
FIELDS = 6
FLUX_LANE = 40
FIELD_LANE = 80
VMEM_BYTES = 48 * 1024 * 1024


def lanes_of(shape):
    return lax.broadcasted_iota(jnp.int32, shape, len(shape) - 1)


def rows_of(shape):
    return lax.broadcasted_iota(jnp.int32, shape, len(shape) - 2)


def roll_lanes(x, amount):
    amount = amount % x.shape[-1] if isinstance(amount, int) else amount
    return x if isinstance(amount, int) and amount == 0 else pltpu.roll(x, amount, x.ndim - 1)


def roll_rows(x, amount):
    return pltpu.roll(x, amount % x.shape[-2], x.ndim - 2)


def coriolis_of(shape, row_start, total_rows):
    rows = (rows_of(shape) + row_start).astype(jnp.float32)
    return 0.3 + 0.4 * rows / total_rows


def edges_kernel(
    total_rows,
    thermal,
    current,
    surface,
    transport,
    flag,
    wet,
    to_west,
    to_east,
    to_north,
    to_south,
    packed,
    sums,
    loads,
):
    depth, ny, nx = thermal.shape
    shape = (ny, nx)
    lane = lanes_of(shape)
    row = rows_of(shape)
    levels = flag[...] * wet[...]
    zero = jnp.zeros(shape, jnp.float32)
    packed[...] = zero
    to_north[6 * W :, :] = jnp.zeros((to_north.shape[0] - 6 * W, nx), jnp.float32)
    to_south[6 * W :, :] = jnp.zeros((to_south.shape[0] - 6 * W, nx), jnp.float32)
    pad = -(-depth // 8) * 8
    p_row, f_row = 6 * W, 6 * W + pad
    for i in range(5):
        loads[i] = zero

    def level(k, carry):
        mask = levels > k
        t = jnp.where(mask, thermal[k], 0.0)
        u = current[0, k]
        v = current[1, k]
        loads[0] += jnp.where(mask, u, 0.0)
        loads[1] += jnp.where(mask, v, 0.0)
        p = loads[2] + t
        loads[2] = p
        east = u * t
        north = v * t
        ahead = jnp.where(lane == nx - 1, 0.0, roll_lanes(p, nx - 1))
        behind = jnp.where(lane == 0, 0.0, roll_lanes(p, 1))
        loads[3] += jnp.where(mask, ahead - behind, 0.0)
        above = jnp.where(row == ny - 1, 0.0, roll_rows(p, ny - 1))
        below = jnp.where(row == 0, 0.0, roll_rows(p, 1))
        loads[4] += jnp.where(mask, above - below, 0.0)
        pair = lane >> 1
        packed[...] = jnp.where(
            pair == k,
            roll_lanes(p, 2 * k + 1),
            jnp.where(pair == k + FLUX_LANE // 2, roll_lanes(east, FLUX_LANE + 2 * k + 1), packed[...]),
        )
        to_north[pl.ds(p_row + k, 1), :] = p[ny - 1 :]
        to_south[pl.ds(p_row + k, 1), :] = p[:1]
        to_north[pl.ds(f_row + k, 1), :] = north[ny - 1 :]
        to_south[pl.ds(f_row + k, 1), :] = north[:1]
        return carry

    lax.fori_loop(0, depth, level, 0)
    scale = TIMESTEP / depth
    slope = 0.5 * THERMAL_EXPANSION
    f = coriolis_of(shape, lax.axis_index("gy") * ny, total_rows)
    forcing_east = scale * (f * loads[1] - slope * loads[3])
    forcing_north = scale * (-f * loads[0] - slope * loads[4])
    sums[0] = loads[0]
    sums[1] = loads[1]
    sums[2] = forcing_east
    sums[3] = forcing_north
    fields = [
        surface[...],
        transport[0],
        transport[1],
        levels.astype(jnp.float32),
        forcing_east,
        forcing_north,
    ]
    pack = packed[...]
    west = roll_lanes(pack, nx - 1)
    east = roll_lanes(pack, 1)
    for i, field in enumerate(fields):
        place = FIELD_LANE + W * i
        mine = (lane >= place) & (lane < place + W)
        west = jnp.where(mine, roll_lanes(field, place), west)
        east = jnp.where(mine, roll_lanes(field, place - (nx - W)), east)
        to_north[W * i : W * (i + 1), :] = field[ny - W :]
        to_south[W * i : W * (i + 1), :] = field[:W]
    to_west[:ny, :] = west
    to_east[:ny, :] = east
    small = lanes_of((8, nx))
    west = jnp.zeros((8, nx), jnp.float32)
    east = west
    for side, ref in enumerate((to_south, to_north)):
        for group in range(pad // 8):
            place = pad * side + 8 * group
            mine = (small >= place) & (small < place + W)
            block = ref[p_row + 8 * group : p_row + 8 * (group + 1), :]
            west = jnp.where(mine, roll_lanes(block, place), west)
            east = jnp.where(mine, roll_lanes(block, place - (nx - W)), east)
    to_west[ny:, :] = west
    to_east[ny:, :] = east
    base = f_row + pad
    to_north[base:, :] = pack[ny - 8 :]
    to_south[base:, :] = pack[:8]


def column_sum(values, levels, parity):
    lane = lanes_of(values.shape)
    use = ((lane & 1) == parity) & (lane < FLUX_LANE) & ((lane >> 1).astype(jnp.float32) < levels)
    return jnp.sum(jnp.where(use, values, 0.0), axis=1, keepdims=True)


def row_sum(values, levels):
    use = rows_of(values.shape).astype(jnp.float32) < levels
    return jnp.sum(jnp.where(use, values, 0.0), axis=0, keepdims=True)


def unfold_rows(east_block, west_block, side, pad):
    nx = east_block.shape[1]
    lane = lanes_of(east_block.shape)
    out = []
    for group in range(pad // 8):
        place = pad * side + 8 * group
        out.append(
            jnp.where(
                lane < W,
                roll_lanes(east_block, -place),
                jnp.where(lane >= nx - W, roll_lanes(west_block, nx - W - place), 0.0),
            )
        )
    return jnp.concatenate(out, axis=0)


def subcycles(surface, transport, levels, sums, packed, from_west, from_east, from_south, from_north, own_north, own_south, pad):
    ny, nx = surface.shape
    p_row = 6 * W
    base = p_row + 2 * pad + 8
    west = jnp.concatenate([from_south[base : base + 8], from_west[:ny], from_north[base : base + 8]], axis=0)
    east = jnp.concatenate([from_south[base + 16 : base + 24], from_east[:ny], from_north[base + 16 : base + 24]], axis=0)
    mine = jnp.concatenate([from_south[base - 8 : base], packed, from_north[base - 8 : base]], axis=0)
    lane = lanes_of(west.shape)
    row = rows_of(west.shape)
    centres = []
    halos = []
    for i, field in enumerate([surface, transport[0], transport[1], levels.astype(jnp.float32), sums[2], sums[3]]):
        place = FIELD_LANE + W * i
        centres.append(jnp.concatenate([from_south[W * i : W * (i + 1)], field, from_north[W * i : W * (i + 1)]], axis=0))
        halos.append(
            jnp.where(
                lane < W,
                roll_lanes(east, -place),
                jnp.where(lane >= nx - W, roll_lanes(west, nx - W - place), 0.0),
            )
        )
    depth_centre, depth_halo = centres[3], halos[3]
    share = TIMESTEP / 20.0 * 0.5 * THERMAL_EXPANSION
    centres[4] = (
        centres[4]
        - jnp.where(lane == nx - 1, share * column_sum(east, depth_centre[:, nx - 1 :], 0), 0.0)
        + jnp.where(lane == 0, share * column_sum(west, depth_centre[:, :1], 1), 0.0)
    )
    halos[4] = (
        halos[4]
        + jnp.where(lane == 0, share * column_sum(mine, depth_halo[:, :1], 0), 0.0)
        - jnp.where(lane == nx - 1, share * column_sum(mine, depth_halo[:, nx - 1 :], 1), 0.0)
    )
    north_beyond = (
        from_north[p_row : p_row + pad],
        unfold_rows(from_north[base + 24 : base + 32], from_north[base + 8 : base + 16], 0, pad),
    )
    south_beyond = (
        from_south[p_row : p_row + pad],
        unfold_rows(from_south[base + 24 : base + 32], from_south[base + 8 : base + 16], 1, pad),
    )
    north_edge = (own_north, unfold_rows(from_east[ny:], from_west[ny:], 1, pad))
    south_edge = (own_south, unfold_rows(from_east[ny:], from_west[ny:], 0, pad))
    for part, fields, depths in ((0, centres, depth_centre), (1, halos, depth_halo)):
        top, bottom = W + ny - 1, W
        fields[5] = (
            fields[5]
            - jnp.where(row == top, share * row_sum(north_beyond[part], depths[top : top + 1]), 0.0)
            + jnp.where(row == bottom, share * row_sum(south_beyond[part], depths[bottom : bottom + 1]), 0.0)
            + jnp.where(row == top + 1, share * row_sum(north_edge[part], depths[top + 1 : top + 2]), 0.0)
            - jnp.where(row == bottom - 1, share * row_sum(south_edge[part], depths[bottom - 1 : bottom]), 0.0)
        )
    height, east_bar, north_bar, water, force_east, force_north = [
        jnp.concatenate([c, h], axis=1) for c, h in zip(centres, halos)
    ]
    wetness = jnp.where(water > 0.0, 1.0, 0.0)
    pull = (0.5 * SUBSTEP * GRAVITY / 20.0) * water
    push_east = SUBSTEP * wetness * force_east
    push_north = SUBSTEP * wetness * force_north
    spread = 0.5 * SUBSTEP * wetness
    cells, lines = height.shape[1], height.shape[0]
    for _ in range(NSUB):
        east_bar = wetness * east_bar + push_east - pull * (roll_lanes(height, cells - 1) - roll_lanes(height, 1))
        north_bar = wetness * north_bar + push_north - pull * (roll_rows(height, lines - 1) - roll_rows(height, 1))
        height = height - spread * (
            (roll_lanes(east_bar, cells - 1) - roll_lanes(east_bar, 1))
            + (roll_rows(north_bar, lines - 1) - roll_rows(north_bar, 1))
        )
    inner = slice(W, W + ny)
    return (
        height[inner, :nx],
        east_bar[inner, :nx],
        north_bar[inner, :nx],
        centres[4][inner],
        centres[5][inner],
    )


def finish_kernel(
    total_rows,
    thermal,
    current,
    mixing,
    surface,
    transport,
    flag,
    wet,
    sums,
    packed,
    own_north,
    own_south,
    from_west,
    from_east,
    from_south,
    from_north,
    mixed,
    velocity,
    height_out,
    transport_out,
    ratios,
    values,
    planes,
):
    depth, ny, nx = thermal.shape
    shape = (ny, nx)
    pad = -(-depth // 8) * 8
    p_row, f_row = 6 * W, 6 * W + pad
    levels = flag[...] * wet[...]
    height, east_bar, north_bar, force_east, force_north = subcycles(
        surface[...],
        (transport[0], transport[1]),
        levels,
        (sums[0], sums[1], sums[2], sums[3]),
        packed[...],
        from_west[...],
        from_east[...],
        from_south[...],
        from_north[...],
        own_north[p_row : p_row + pad],
        own_south[p_row : p_row + pad],
        pad,
    )
    height_out[...] = height
    transport_out[0] = east_bar
    transport_out[1] = north_bar
    count = jnp.maximum(levels.astype(jnp.float32), 1.0)
    planes[0] = east_bar - (sums[0] + depth * force_east) / count
    planes[1] = north_bar - (sums[1] + depth * force_north) / count
    lane = lanes_of(shape)
    row = rows_of(shape)
    planes[2] = jnp.where((lane & 1) == 0, from_east[:ny], from_west[:ny])
    planes[3] = jnp.zeros(shape, jnp.float32)
    planes[4] = TIMESTEP * coriolis_of(shape, lax.axis_index("gy") * ny, total_rows)
    slope = 0.5 * TIMESTEP * THERMAL_EXPANSION

    def ahead_less_behind(x, halo):
        return jnp.where(lane == nx - 1, halo, roll_lanes(x, nx - 1)) - jnp.where(lane == 0, halo, roll_lanes(x, 1))

    def above_less_below(x, above, below):
        return jnp.where(row == ny - 1, above, roll_rows(x, ny - 1)) - jnp.where(row == 0, below, roll_rows(x, 1))

    def forward(k, carry):
        mask = levels > k
        raw = thermal[k]
        t = jnp.where(mask, raw, 0.0)
        u = current[0, k]
        v = current[1, k]
        p = planes[3] + t
        planes[3] = p
        dx = ahead_less_behind(p, roll_lanes(planes[2], nx - 1 - 2 * k))
        dy = above_less_below(p, from_north[pl.ds(p_row + k, 1), :], from_south[pl.ds(p_row + k, 1), :])
        turn = planes[4]
        velocity[0, k] = jnp.where(mask, u + turn * v - slope * dx + planes[0], 0.0)
        velocity[1, k] = jnp.where(mask, v - turn * u - slope * dy + planes[1], 0.0)
        spread = ahead_less_behind(u * t, roll_lanes(planes[2], nx - 1 - FLUX_LANE - 2 * k)) + above_less_below(
            v * t, from_north[pl.ds(f_row + k, 1), :], from_south[pl.ds(f_row + k, 1), :]
        )
        source = jnp.where(mask, raw - 0.5 * TRANSPORT_SPEED * spread, 0.0)
        below = jnp.minimum(k + 1, depth - 1)
        upper = jnp.where((levels > k + 1) & (k < depth - 1), 0.5 * MIXING * (mixing[k] + mixing[below]), 0.0)
        lower = planes[5]
        planes[5] = upper
        above = jnp.maximum(k - 1, 0)
        inverse = 1.0 / (1.0 + upper + lower * (1.0 + ratios[above]))
        ratios[k] = -upper * inverse
        values[k] = (source + lower * values[above]) * inverse
        return carry

    planes[5] = jnp.zeros(shape, jnp.float32)
    ratios[0] = jnp.zeros(shape, jnp.float32)
    values[0] = jnp.zeros(shape, jnp.float32)
    lax.fori_loop(0, depth, forward, 0)
    mixed[depth - 1] = values[depth - 1]

    def backward(i, carry):
        k = depth - 2 - i
        mixed[k] = values[k] - ratios[k] * mixed[k + 1]
        return carry

    lax.fori_loop(0, depth - 1, backward, 0)


def shift(block, dx, dy):
    sx, sy, sa = (lax.axis_size(a) for a in AXES)
    pairs = []
    for x in range(sx * sa):
        for y in range(sy):
            tx, ty = (x + dx) % (sx * sa), y + dy
            if 0 <= ty < sy:
                source = (x // sa * sy + y) * sa + x % sa
                pairs.append((source, (tx // sa * sy + ty) * sa + tx % sa))
    return lax.ppermute(block, AXES, pairs)


def per_device(thermal, current, mixing, surface, transport, flag, wet):
    depth, ny, nx = thermal.shape
    total_rows = ny * lax.axis_size("gy")
    pad = -(-depth // 8) * 8
    f32 = jnp.float32
    whole = pl.BlockSpec(memory_space=pltpu.VMEM)
    params = pltpu.CompilerParams(vmem_limit_bytes=VMEM_BYTES)
    rows = 6 * W + 2 * pad + 8
    to_west, to_east, to_north, to_south, packed, sums = pl.pallas_call(
        functools.partial(edges_kernel, total_rows),
        out_shape=[
            jax.ShapeDtypeStruct((ny + 8, nx), f32),
            jax.ShapeDtypeStruct((ny + 8, nx), f32),
            jax.ShapeDtypeStruct((rows, nx), f32),
            jax.ShapeDtypeStruct((rows, nx), f32),
            jax.ShapeDtypeStruct((ny, nx), f32),
            jax.ShapeDtypeStruct((4, ny, nx), f32),
        ],
        in_specs=[whole] * 6,
        out_specs=[whole] * 6,
        scratch_shapes=[pltpu.VMEM((5, ny, nx), f32)],
        compiler_params=params,
        name="edges",
    )(thermal, current, surface, transport, flag, wet)
    from_west = shift(to_east, 1, 0)
    from_east = shift(to_west, -1, 0)
    north = jnp.concatenate([to_north, from_west[ny - 8 :], from_east[ny - 8 :]], axis=0)
    south = jnp.concatenate([to_south, from_west[:8], from_west[ny:], from_east[:8], from_east[ny:]], axis=0)
    from_south = shift(north, 0, 1)
    from_north = shift(south, 0, -1)
    return pl.pallas_call(
        functools.partial(finish_kernel, total_rows),
        out_shape=[
            jax.ShapeDtypeStruct((depth, ny, nx), f32),
            jax.ShapeDtypeStruct((2, depth, ny, nx), f32),
            jax.ShapeDtypeStruct((ny, nx), f32),
            jax.ShapeDtypeStruct((2, ny, nx), f32),
        ],
        in_specs=[whole] * 15,
        out_specs=[whole] * 4,
        scratch_shapes=[
            pltpu.VMEM((depth, ny, nx), f32),
            pltpu.VMEM((depth, ny, nx), f32),
            pltpu.VMEM((6, ny, nx), f32),
        ],
        compiler_params=params,
        name="finish",
    )(
        thermal,
        current,
        mixing,
        surface,
        transport,
        flag,
        wet,
        sums,
        packed,
        to_north,
        to_south,
        from_west,
        from_east,
        from_south,
        from_north,
    )


def solution(mesh):
    placed = (
        P(None, "gy", ("gx", "ga")),
        P(None, None, "gy", ("gx", "ga")),
        P(None, "gy", ("gx", "ga")),
        P("gy", ("gx", "ga")),
        P(None, "gy", ("gx", "ga")),
        P("gy", ("gx", "ga")),
        P("gy", ("gx", "ga")),
    )
    return jax.shard_map(
        per_device,
        mesh=mesh,
        in_specs=placed,
        out_specs=(
            P(None, "gy", ("gx", "ga")),
            P(None, None, "gy", ("gx", "ga")),
            P("gy", ("gx", "ga")),
            P(None, "gy", ("gx", "ga")),
        ),
        check_vma=False,
    )
```

time: 219 us -> 46.2 us (0.21)
  the two profiles are of different devices: /device:TPU:33 before, /device:TPU:1 now
where the time goes in v1:
time: 46.2 us; the launch traced here: 45.9 us
  starting transfers between devices  16.1 us (35%)
  Pallas kernels  13 us (28%)
  waiting for transfers between devices  9.57 us (21%)
  local copies, waits for them, and re-layouts  6.5 us (14%)
  between operations  0.72 us (2%)
    ppermute x4, starting transfers between devices, shift(): return lax.ppermute(block, AXES, pairs)  16.1 us
    pallas_call x1, Pallas kernels, per_device(): pl.pallas_call(functools.partial(finish_kernel, total_rows), out_shape=[j...  9.66 us
    ppermute x4, waiting for transfers between devices, shift(): return lax.ppermute(block, AXES, pairs)  9.57 us
    unnamed x18, local copies, waits for them, and re-layouts  6.49 us
    pallas_call x1, Pallas kernels, per_device(): pl.pallas_call(functools.partial(edges_kernel, total_rows), out_shape=[ja...  3.3 us
  transfers between devices with their start and end apart: 4, of which 3 were waited for; matrix products, arithmetic and copies ran while one was open for 0% of the time, Pallas kernels for 0%

profile of v1, /device:TPU:1, one launch (start us, length us, event | category | flops | bytes accessed | tf_op | source)
XLA Modules:
  0.0 45.9 jit_solution(7509140352440613735)
XLA Ops:
  0.6 0.0 copy-start
  0.6 1.7 %copy-done = f32[2,20,128,128]{3,2,1,0:T(8,128)S(1)} copy-done((f32[2,20,128,128]{3,2,1,0:T(8,128)S(1)}, f32[2,20,128,128]{3,2,1,0:T(8,128)}, u32[]{:S(2)}) %copy-start) | copy-done | bytes 2621464
  2.4 0.0 copy-start.1
  2.4 1.3 %copy-done.1 = f32[20,128,128]{2,1,0:T(8,128)S(1)} copy-done((f32[20,128,128]{2,1,0:T(8,128)S(1)}, f32[20,128,128]{2,1,0:T(8,128)}, u32[]{:S(2)}) %copy-start.1) | copy-done | bytes 1310744
  3.7 0.0 copy-start.3
  3.7 0.9 %copy-done.3 = f32[2,128,128]{2,1,0:T(8,128)S(1)} copy-done((f32[2,128,128]{2,1,0:T(8,128)S(1)}, f32[2,128,128]{2,1,0:T(8,128)}, u32[]{:S(2)}) %copy-start.3) | copy-done | bytes 131096
  4.6 0.0 copy-start.4
  4.6 0.8 %copy-done.4 = f32[128,128]{1,0:T(8,128)S(1)} copy-done((f32[128,128]{1,0:T(8,128)S(1)}, f32[128,128]{1,0:T(8,128)}, u32[]{:S(2)}) %copy-start.4) | copy-done | bytes 65560
  5.4 0.0 copy-start.5
  5.4 0.8 %copy-done.5 = s32[128,128]{1,0:T(8,128)S(1)} copy-done((s32[128,128]{1,0:T(8,128)S(1)}, s32[128,128]{1,0:T(8,128)}, u32[]{:S(2)}) %copy-start.5) | copy-done | bytes 65560
  6.3 0.0 copy-start.6
  6.3 0.8 %copy-done.6 = s32[128,128]{1,0:T(8,128)S(1)} copy-done((s32[128,128]{1,0:T(8,128)S(1)}, s32[128,128]{1,0:T(8,128)}, u32[]{:S(2)}) %copy-start.6) | copy-done | bytes 65560
  7.1 0.0 copy-start.2
  7.1 3.3 %edges.1 = (f32[136,128]{1,0:T(8,128)S(1)}, f32[136,128]{1,0:T(8,128)S(1)}, f32[104,128]{1,0:T(8,128)S(1)}, f32[104,128]{1,0:T(8,128)S(1)}, f32[128,128]{1,0:T(8,128)S(1)}, /*index=5*/f32[4,128,128]{2,1,0:T(8,128)S(1)}) custom-call(f32[20,128,128]{2,1,0:T(8,128)S(1)} %copy-done.1, f32[2,20,128,128]{3,2,1,0:T(8,128)S(1)} %copy-done, ...), custom_call_target="tpu_custom_call" | custom-call | tf_op jit(solution)/shard_map/edges/pallas_call | solution.py:383
  10.4 7.8 %collective-permute-start = (f32[136,128]{1,0:T(8,128)S(1)}, f32[136,128]{1,0:T(8,128)S(1)}, u32[]{:S(2)}, u32[]{:S(2)}) collective-permute-start(f32[136,128]{1,0:T(8,128)S(1)} %get-tuple-element.14), channel_id=1, source_target_pairs={{0,1},{2,3},{4,5},{6,7},{8,9},{10,11},{12,13},{14,15},{1,16},{3,18... | collective-permute-start | bytes 208904 | tf_op jit(solution)/shard_map/ppermute | solution.py:372
  18.2 1.2 %collective-permute-start.1 = (f32[136,128]{1,0:T(8,128)S(1)}, f32[136,128]{1,0:T(8,128)S(1)}, u32[]{:S(2)}, u32[]{:S(2)}) collective-permute-start(f32[136,128]{1,0:T(8,128)S(1)} %get-tuple-element.15), channel_id=1, source_target_pairs={{0,241},{2,243},{4,245},{6,247},{8,249},{10,251},{12,253},{14,255}... | collective-permute-start | bytes 208904 | tf_op jit(solution)/shard_map/ppermute | solution.py:372
  19.4 1.6 %collective-permute-done.from_west = f32[136,128]{1,0:T(8,128)S(1)} collective-permute-done((f32[136,128]{1,0:T(8,128)S(1)}, f32[136,128]{1,0:T(8,128)S(1)}, u32[]{:S(2)}, u32[]{:S(2)}) %collective-permute-start) | collective-permute-done | bytes 69664 | tf_op jit(solution)/shard_map/ppermute | solution.py:372
  21.1 4.3 %collective-permute-done.1.from_east = f32[136,128]{1,0:T(8,128)S(1)} collective-permute-done((f32[136,128]{1,0:T(8,128)S(1)}, f32[136,128]{1,0:T(8,128)S(1)}, u32[]{:S(2)}, u32[]{:S(2)}) %collective-permute-start.1) | collective-permute-done | bytes 69664 | tf_op jit(solution)/shard_map/ppermute | solution.py:372
  25.3 5.2 %collective-permute-start.2 = (f32[136,128]{1,0:T(8,128)S(1)}, f32[136,128]{1,0:T(8,128)S(1)}, u32[]{:S(2)}, u32[]{:S(2)}) collective-permute-start(f32[136,128]{1,0:T(8,128)S(1)} %pad_maximum_fusion), channel_id=1, source_target_pairs={{0,2},{2,4},{4,6},{6,8},{8,10},{10,12},{12,14},{1,3},{3,5},{5,7},{... | collective-permute-start | bytes 208904 | tf_op jit(solution)/shard_map/ppermute | solution.py:372
  30.6 1.9 %collective-permute-start.3 = (f32[136,128]{1,0:T(8,128)S(1)}, f32[136,128]{1,0:T(8,128)S(1)}, u32[]{:S(2)}, u32[]{:S(2)}) collective-permute-start(f32[136,128]{1,0:T(8,128)S(1)} %constant_dynamic-update-slice_fusion), channel_id=1, source_target_pairs={{2,0},{4,2},{6,4},{8,6},{10,8},{12,10},{14,12},{3,1},{5,3},{7,5},{... | collective-permute-start | bytes 208904 | tf_op jit(solution)/shard_map/ppermute | solution.py:372
  32.5 0.0 collective-permute-done.2.from_south
  32.5 3.7 %collective-permute-done.3.from_north = f32[136,128]{1,0:T(8,128)S(1)} collective-permute-done((f32[136,128]{1,0:T(8,128)S(1)}, f32[136,128]{1,0:T(8,128)S(1)}, u32[]{:S(2)}, u32[]{:S(2)}) %collective-permute-start.3) | collective-permute-done | bytes 69664 | tf_op jit(solution)/shard_map/ppermute | solution.py:372
  36.2 0.0 copy-done.2
  36.2 9.7 %finish.1 = (f32[20,128,128]{2,1,0:T(8,128)}, f32[2,20,128,128]{3,2,1,0:T(8,128)}, f32[128,128]{1,0:T(8,128)}, f32[2,128,128]{2,1,0:T(8,128)}) custom-call(f32[20,128,128]{2,1,0:T(8,128)S(1)} %copy-done.1, f32[2,20,128,128]{3,2,1,0:T(8,128)} %current.3, f32[20,128,128]{2,1,0:T(8,128)S(1)} %copy-done.2, f32[128,128]{1,0:T(8,128)S(1)} %copy-done.4, ...), custom_call_target="tpu_custom_call" | custom-call | tf_op jit(solution)/shard_map/finish/pallas_call | solution.py:405
  (8 shorter events, 0.0 us)
Async XLA Ops:
  0.6 1.7 %copy-start = (f32[2,20,128,128]{3,2,1,0:T(8,128)S(1)}, f32[2,20,128,128]{3,2,1,0:T(8,128)}, u32[]{:S(2)}) copy-start(f32[2,20,128,128]{3,2,1,0:T(8,128)} %current.3) | copy-start | bytes 7864324
  2.4 1.3 %copy-start.1 = (f32[20,128,128]{2,1,0:T(8,128)S(1)}, f32[20,128,128]{2,1,0:T(8,128)}, u32[]{:S(2)}) copy-start(f32[20,128,128]{2,1,0:T(8,128)} %thermal.3) | copy-start | bytes 3932164
  3.7 0.9 %copy-start.3 = (f32[2,128,128]{2,1,0:T(8,128)S(1)}, f32[2,128,128]{2,1,0:T(8,128)}, u32[]{:S(2)}) copy-start(f32[2,128,128]{2,1,0:T(8,128)} %transport.3) | copy-start | bytes 393220
  4.6 0.8 %copy-start.4 = (f32[128,128]{1,0:T(8,128)S(1)}, f32[128,128]{1,0:T(8,128)}, u32[]{:S(2)}) copy-start(f32[128,128]{1,0:T(8,128)} %surface.3) | copy-start | bytes 196612
  5.4 0.8 %copy-start.5 = (s32[128,128]{1,0:T(8,128)S(1)}, s32[128,128]{1,0:T(8,128)}, u32[]{:S(2)}) copy-start(s32[128,128]{1,0:T(8,128)} %flag.3) | copy-start | bytes 196612
  6.3 0.8 %copy-start.6 = (s32[128,128]{1,0:T(8,128)S(1)}, s32[128,128]{1,0:T(8,128)}, u32[]{:S(2)}) copy-start(s32[128,128]{1,0:T(8,128)} %wet.3) | copy-start | bytes 196612
  7.1 29.1 %copy-start.2 = (f32[20,128,128]{2,1,0:T(8,128)S(1)}, f32[20,128,128]{2,1,0:T(8,128)}, u32[]{:S(2)}) copy-start(f32[20,128,128]{2,1,0:T(8,128)} %mixing.1) | copy-start | bytes 3932164
  10.4 10.6 %collective-permute-start = (f32[136,128]{1,0:T(8,128)S(1)}, f32[136,128]{1,0:T(8,128)S(1)}, u32[]{:S(2)}, u32[]{:S(2)}) collective-permute-start(f32[136,128]{1,0:T(8,128)S(1)} %get-tuple-element.14), channel_id=1, source_target_pairs={{0,1},{2,3},{4,5},{6,7},{8,9},{10,11},{12,13},{14,15},{1,16},{3,18... | collective-permute-start | bytes 208904 | tf_op jit(solution)/shard_map/ppermute | solution.py:372
  18.2 7.1 %collective-permute-start.1 = (f32[136,128]{1,0:T(8,128)S(1)}, f32[136,128]{1,0:T(8,128)S(1)}, u32[]{:S(2)}, u32[]{:S(2)}) collective-permute-start(f32[136,128]{1,0:T(8,128)S(1)} %get-tuple-element.15), channel_id=1, source_target_pairs={{0,241},{2,243},{4,245},{6,247},{8,249},{10,251},{12,253},{14,255}... | collective-permute-start | bytes 208904 | tf_op jit(solution)/shard_map/ppermute | solution.py:372
  25.3 7.1 %collective-permute-start.2 = (f32[136,128]{1,0:T(8,128)S(1)}, f32[136,128]{1,0:T(8,128)S(1)}, u32[]{:S(2)}, u32[]{:S(2)}) collective-permute-start(f32[136,128]{1,0:T(8,128)S(1)} %pad_maximum_fusion), channel_id=1, source_target_pairs={{0,2},{2,4},{4,6},{6,8},{8,10},{10,12},{12,14},{1,3},{3,5},{5,7},{... | collective-permute-start | bytes 208904 | tf_op jit(solution)/shard_map/ppermute | solution.py:372
  30.6 5.6 %collective-permute-start.3 = (f32[136,128]{1,0:T(8,128)S(1)}, f32[136,128]{1,0:T(8,128)S(1)}, u32[]{:S(2)}, u32[]{:S(2)}) collective-permute-start(f32[136,128]{1,0:T(8,128)S(1)} %constant_dynamic-update-slice_fusion), channel_id=1, source_target_pairs={{2,0},{4,2},{6,4},{8,6},{10,8},{12,10},{14,12},{3,1},{5,3},{7,5},{... | collective-permute-start | bytes 208904 | tf_op jit(solution)/shard_map/ppermute | solution.py:372
